TPU v7x, 32 devices: a whole 2x2x4 slice. The times are simulated.
32 devices in a mesh: parts: 2 (over y), warp: 4 (over z), weft: 2 (over x), ply: 2 (over core).
Axes of the slice: x: 2, y: 2, z: 4, core: 2. Of those that a mesh axis runs over, the one named last changes fastest.
Arguments:
- lam_start: float32 [64, 256, 512], P(('parts', 'warp', 'ply'), 'weft'), parts along dimension 0, as said below
- resid_start: float32 [64, 256, 512], P(('parts', 'warp', 'ply'), 'weft'), parts along dimension 0, as said below
- dirn_start: float32 [64, 256, 512], P(('parts', 'warp', 'ply'), 'weft'), parts along dimension 0, as said below
- rz_start: float32 [2], P('parts'), parts along dimension 0, may hold values from 10485760 to 83886080
- pattern: int32 [64, 256], P(('parts', 'warp', 'ply'), 'weft'), parts along dimension 0, may hold values from 0 to 2
- corners: int32 [4, 64, 256], P(None, ('parts', 'warp', 'ply'), 'weft'), parts along dimension 1, may hold values from -1 to 127, as said below
- schur_inv: float32 [3, 512, 512], replicated, as said below
- schur_dirichlet: float32 [3, 512, 512], replicated, as said below
- corner_shape: float32 [3, 4, 512], replicated, may hold values from -0.3 to 0.3
- coarse_inv: float32 [256, 128], P(('parts', 'warp', 'weft', 'ply')), parts along dimension 0, as said below
Outputs:
- lam_final: float32 [64, 256, 512], P(('parts', 'warp', 'ply'), 'weft'), parts along dimension 0
- resid_final: float32 [64, 256, 512], P(('parts', 'warp', 'ply'), 'weft'), parts along dimension 0
- dirn_final: float32 [64, 256, 512], P(('parts', 'warp', 'ply'), 'weft'), parts along dimension 0
There are 2 independent parts, one for each index of `parts`. A program takes and returns all parts, laid end to end along the dimension named above; an argument that names none is the same for every part. Nothing has to cross between parts.
Inputs may be any that keep to these rules, and one draw needn't show every extreme that they name: `lam_start`: in each cell the W block is minus the E block of the cell to its west and zero where j = 0; the S block is minus the N block of the cell to its south and zero where i = 0. `resid_start`: in each cell the W block is minus the E block of the cell to its west and zero where j = 0; the S block is minus the N block of the cell to its south and zero where i = 0. `dirn_start`: in each cell the W block is minus the E block of the cell to its west and zero where j = 0; the S block is minus the N block of the cell to its south and zero where i = 0. `corners`: corner k of cell (i, j) is the corner node (i, j), (i, j + 1), (i + 1, j) or (i + 1, j + 1) for k = 0, 1, 2, 3; nodes (a, b) with a = 32 or b = 256 are -1; every other node's row is that of its aggregate, the block of 8 x 8 nodes with the same a // 8 and b // 8; each aggregate has its own row, and which aggregate has which row is drawn. `schur_inv`: each matrix is symmetric positive definite. `schur_dirichlet`: each matrix is symmetric positive definite. `coarse_inv`: symmetric positive definite.
All inputs are finite; a program needn't handle non-finite values.
Results may differ from a plain program's by a relative error of at most 0.00027.
Values sent between devices are 32-bit elements; how exact they have to be, the bound alone decides.
A program may use at most 64 MiB of HBM per device.

v0:
```python
import jax
import jax.numpy as jnp
from jax import lax
from jax.sharding import PartitionSpec as P

ITERS = 3


HIGHEST = lax.Precision.HIGHEST


def with_halo(array, sides, width):
    for axis, dim in sides:
        count, length = (lax.axis_size(axis), array.shape[dim])
        up = [(i, (i + 1) % count) for i in range(count - 1)]
        down = [(j, i) for i, j in up]
        last = lax.slice_in_dim(array, length - width, length, axis=dim)
        leading = lax.slice_in_dim(array, 0, width, axis=dim)
        before = lax.ppermute(last, axis, up)
        after = lax.ppermute(leading, axis, down)
        array = jnp.concatenate([before, array, after], axis=dim)
    return array


def split_edges(values, edge_len):
    return (
        values[..., :edge_len],
        values[..., edge_len : 2 * edge_len],
        values[..., 2 * edge_len : 3 * edge_len],
        values[..., 3 * edge_len :],
    )


def cross_faces(values, edge_len, west_keep, south_keep):
    west_side, east_side, south_side, north_side = split_edges(values, edge_len)
    rows_here, cols_here = (values.shape[0], values.shape[1])
    local_row = lax.broadcasted_iota(jnp.int32, (rows_here, cols_here, 1), 0)
    local_col = lax.broadcasted_iota(jnp.int32, (rows_here, cols_here, 1), 1)
    along_rows = jnp.where(local_row == 0, south_side, north_side)
    along_cols = jnp.where(local_col == 0, west_side, east_side)
    padded = with_halo(
        jnp.concatenate([along_rows, along_cols], axis=2), ((("warp", "ply"), 0), ("weft", 1)), 1
    )
    from_south = padded[0, 1:-1, :edge_len]
    from_north = padded[-1, 1:-1, :edge_len]
    from_west = padded[1:-1, 0, edge_len:]
    from_east = padded[1:-1, -1, edge_len:]
    east_west = jnp.concatenate([west_side[:, 1:], from_east[:, None]], axis=1)
    west_east = jnp.concatenate([from_west[:, None], east_side[:, :-1]], axis=1)
    north_south = jnp.concatenate([south_side[1:], from_north[None]], axis=0)
    south_north = jnp.concatenate([from_south[None], north_side[:-1]], axis=0)
    return jnp.concatenate(
        [
            (west_side - west_east) * west_keep,
            east_side - east_west,
            (south_side - south_north) * south_keep,
            north_side - north_south,
        ],
        axis=2,
    )


def apply_cells(rows_flat, matrices, cell_order, inverse, group_sizes):
    sorted_rows = rows_flat[cell_order]
    product = lax.ragged_dot(
        sorted_rows, matrices, group_sizes, precision=HIGHEST, preferred_element_type=jnp.float32
    )
    return product[inverse]


def on_device(
    lam_start,
    resid_start,
    dirn_start,
    rz_start,
    pattern,
    corners,
    schur_inv,
    schur_dirichlet,
    corner_shape,
    coarse_inv,
):
    rows_here, cols_here, dof_count = lam_start.shape
    edge_len = dof_count // 4
    pattern_count = schur_inv.shape[0]
    coarse_count = coarse_inv.shape[1]
    row_pos = (
        lax.broadcasted_iota(jnp.int32, (rows_here, cols_here, 1), 0)
        + lax.axis_index(("warp", "ply")) * rows_here
    )
    col_pos = (
        lax.broadcasted_iota(jnp.int32, (rows_here, cols_here, 1), 1)
        + lax.axis_index("weft") * cols_here
    )
    total_rows = lax.axis_size(("warp", "ply")) * rows_here
    total_cols = lax.axis_size("weft") * cols_here
    west_keep = (col_pos > 0).astype(jnp.float32)
    south_keep = (row_pos > 0).astype(jnp.float32)
    east_weight = jnp.where(col_pos == total_cols - 1, 1.0, 0.5).astype(jnp.float32)
    north_weight = jnp.where(row_pos == total_rows - 1, 1.0, 0.5).astype(jnp.float32)
    block_shape = (rows_here, cols_here, edge_len)
    edge_weight = jnp.concatenate(
        [
            jnp.broadcast_to(0.5 * west_keep, block_shape),
            jnp.broadcast_to(east_weight, block_shape),
            jnp.broadcast_to(0.5 * south_keep, block_shape),
            jnp.broadcast_to(north_weight, block_shape),
        ],
        axis=2,
    )
    cell_kind = pattern.reshape(-1)
    cell_order = jnp.argsort(cell_kind, stable=True)
    inverse = jnp.argsort(cell_order, stable=True)
    selector = (cell_kind[None, :] == jnp.arange(pattern_count, dtype=jnp.int32)[:, None]).astype(
        jnp.float32
    )
    group_sizes = jnp.sum(selector, axis=1).astype(jnp.int32)
    corner_rows = corners.reshape(4, -1)
    corner_live = corner_rows >= 0
    corner_slot = jnp.where(corner_live, corner_rows, coarse_count)
    corner_pick = jnp.where(corner_live, corner_rows, 0)
    multiplier, residual, direction = (lam_start, resid_start, dirn_start)
    rz_prev = rz_start[0]
    for iteration in range(ITERS):
        scaled = (edge_weight * residual).reshape(-1, dof_count)
        spread = apply_cells(scaled, schur_dirichlet, cell_order, inverse, group_sizes).reshape(
            residual.shape
        )
        precond = edge_weight * cross_faces(spread, edge_len, west_keep, south_keep)
        rz_now = lax.psum(jnp.sum(edge_weight * residual * precond), ("warp", "weft", "ply"))
        direction = precond + rz_now / rz_prev * direction
        rows_flat = direction.reshape(-1, dof_count)
        local_image = apply_cells(rows_flat, schur_inv, cell_order, inverse, group_sizes)
        corner_terms = jnp.einsum("pkd,cd->pkc", corner_shape, rows_flat, precision=HIGHEST)
        corner_load = jnp.sum(corner_terms * selector[:, None, :], axis=0)
        partial_rhs = jax.ops.segment_sum(
            corner_load.reshape(-1), corner_slot.reshape(-1), num_segments=coarse_count + 1
        )[:coarse_count]
        coarse_rhs = lax.psum(partial_rhs, ("warp", "weft", "ply"))
        coarse_sol = lax.all_gather(
            jnp.dot(coarse_inv, coarse_rhs, precision=HIGHEST),
            ("warp", "weft", "ply"),
            axis=0,
            tiled=True,
        )
        corner_vals = jnp.where(corner_live, coarse_sol[corner_pick], 0.0)
        full_image = local_image + jnp.einsum(
            "pkc,pkd->cd", selector[:, None, :] * corner_vals[None], corner_shape, precision=HIGHEST
        )
        applied = cross_faces(full_image.reshape(direction.shape), edge_len, west_keep, south_keep)
        curvature = lax.psum(jnp.sum(edge_weight * direction * applied), ("warp", "weft", "ply"))
        alpha_step = rz_now / curvature
        multiplier = multiplier + alpha_step * direction
        residual = residual - alpha_step * applied
        rz_prev = rz_now
    return (multiplier, residual, direction)


def solution(mesh):
    return jax.shard_map(
        on_device,
        mesh=mesh,
        in_specs=(
            P(("parts", "warp", "ply"), "weft", None),
            P(("parts", "warp", "ply"), "weft", None),
            P(("parts", "warp", "ply"), "weft", None),
            P("parts"),
            P(("parts", "warp", "ply"), "weft"),
            P(None, ("parts", "warp", "ply"), "weft"),
            P(),
            P(),
            P(),
            P(("parts", "warp", "weft", "ply"), None),
        ),
        out_specs=(
            P(("parts", "warp", "ply"), "weft", None),
            P(("parts", "warp", "ply"), "weft", None),
            P(("parts", "warp", "ply"), "weft", None),
        ),
        check_vma=False,
    )
```

profile of v0, /device:TPU:0, one launch (start us, length us, event | category | flops | bytes accessed | tf_op | source)
XLA Modules:
  0.0 678.7 jit_solution(7160559662432840204)
XLA Ops:
  3.4 4.4 sort.31
  7.8 3.8 sort.32
  13.5 2.3 gather_fusion
  15.8 8.7 %ragged-dot-none.5 = f32[512,512]{1,0:T(8,128)} custom-call(s32[1]{0:T(128)} %get-tuple-element.27, s32[4]{0:T(128)} %get-tuple-element.28, s32[4]{0:T(128)} %get-tuple-element.29, s32[4]{0:T(128)} %get-tuple-element.30, s32[1]{0:T(128)} %get-tuple-element.27, f32[512,512]{1,0:T(8,128)} %gather_fusion, f32[3,512,512]{2,1,0:T(8,128)} %param.17), custom_call_target="tpu_custom_call" | custom-call | flops 268435456 | bytes 5242892 | tf_op jit(solution)/shard_map/ragged_dot_general/ragged-dot-none
  24.6 3.3 gather_fusion.1
  29.4 3.1 collective-permute-start
  38.5 3.4 collective-permute-start.2
  50.5 33.6 %psum.63 = f32[]{:T(128)} all-reduce(f32[]{:T(128)} %multiply_reduce_fusion.2), channel_id=1, replica_groups=mesh['parts'=2,'warp'=4,'weft'=2,'ply'=2] {'warp','weft','ply'}, use_global_device_ids=true, to_apply=%region_4.5 | all-reduce | flops 1 | bytes 8 | tf_op jit(solution)/shard_map/psum | solution.py:130
  87.2 14.7 %scatter_custom_fusion = f32[129]{0:T(256)S(1)} fusion(s32[2048]{0:T(1024)S(1)} %bitcast.138, f32[2048]{0:T(1024)S(1)} %bitcast.142, f32[]{:T(128)} %constant.17.clone.1), kind=kCustom, calls=%fused_computation.187 | custom fusion | flops 2048 | bytes 520 | tf_op jit(solution)/shard_map/scatter-add | solution.py:136
  101.8 29.5 %psum.64 = f32[128]{0:T(128)S(1)} all-reduce(f32[128]{0:T(128)S(1)} %slice.337), channel_id=1, replica_groups=mesh['parts'=2,'warp'=4,'weft'=2,'ply'=2] {'warp','weft','ply'}, use_global_device_ids=true, to_apply=%region_7.8 | all-reduce | flops 128 | bytes 1024 | tf_op jit(solution)/shard_map/psum | solution.py:139
  131.7 29.5 %all-reduce = f32[128]{0:T(128)S(1)} all-reduce(f32[128]{0:T(128)S(1)} %dynamic-update-slice), channel_id=1, replica_groups=mesh['parts'=2,'warp'=4,'weft'=2,'ply'=2] {'warp','weft','ply'}, use_global_device_ids=true, to_apply=%add | all-reduce | flops 128 | bytes 1024
  161.1 12.6 %gather_fusion.4 = f32[2048]{0:T(1024)S(1)} fusion(f32[128]{0:T(128)S(1)} %all-reduce, s32[2048]{0:T(1024)S(1)} %broadcast_clamp_fusion), kind=kCustom, calls=%fused_computation.4 | custom fusion | bytes 24576 | tf_op jit(solution)/shard_map/gather | solution.py:146
  173.8 2.3 gather_fusion.2
  176.1 8.7 %ragged-dot-none.4 = f32[512,512]{1,0:T(8,128)} custom-call(s32[1]{0:T(128)} %get-tuple-element.27, s32[4]{0:T(128)} %get-tuple-element.28, s32[4]{0:T(128)} %get-tuple-element.29, s32[4]{0:T(128)} %get-tuple-element.30, s32[1]{0:T(128)} %get-tuple-element.27, f32[512,512]{1,0:T(8,128)} %gather_fusion.2, f32[3,512,512]{2,1,0:T(8,128)} %param.16), custom_call_target="tpu_custom_call" | custom-call | flops 268435456 | bytes 5242892 | tf_op jit(solution)/shard_map/ragged_dot_general/ragged-dot-none
  184.8 3.9 gather_fusion.3
  188.8 2.3 fusion
  199.1 4.0 collective-permute-done.7
  205.1 32.0 %psum.65 = f32[]{:T(128)} all-reduce(f32[]{:T(128)} %fusion.23), channel_id=1, replica_groups=mesh['parts'=2,'warp'=4,'weft'=2,'ply'=2] {'warp','weft','ply'}, use_global_device_ids=true, to_apply=%region_9.10 | all-reduce | flops 1 | bytes 8 | tf_op jit(solution)/shard_map/psum | solution.py:151
  240.1 2.3 gather_fusion.5
  242.4 8.7 %ragged-dot-none.3 = f32[512,512]{1,0:T(8,128)} custom-call(s32[1]{0:T(128)} %get-tuple-element.27, s32[4]{0:T(128)} %get-tuple-element.28, s32[4]{0:T(128)} %get-tuple-element.29, s32[4]{0:T(128)} %get-tuple-element.30, s32[1]{0:T(128)} %get-tuple-element.27, f32[512,512]{1,0:T(8,128)} %gather_fusion.5, f32[3,512,512]{2,1,0:T(8,128)} %param.17), custom_call_target="tpu_custom_call" | custom-call | flops 268435456 | bytes 5242892 | tf_op jit(solution)/shard_map/ragged_dot_general/ragged-dot-none
  251.2 3.9 gather_fusion.6
  263.8 4.1 collective-permute-done.11
  270.0 30.6 %psum.66 = f32[]{:T(128)} all-reduce(f32[]{:T(128)} %multiply_reduce_fusion.1), channel_id=1, replica_groups=mesh['parts'=2,'warp'=4,'weft'=2,'ply'=2] {'warp','weft','ply'}, use_global_device_ids=true, to_apply=%region_11.12 | all-reduce | flops 1 | bytes 8 | tf_op jit(solution)/shard_map/psum | solution.py:130
  304.3 14.7 %scatter_custom_fusion.1 = f32[129]{0:T(256)S(1)} fusion(s32[2048]{0:T(1024)S(1)} %bitcast.139, f32[2048]{0:T(1024)S(1)} %bitcast.143, f32[]{:T(128)} %constant.17.clone.1), kind=kCustom, calls=%fused_computation.185 | custom fusion | flops 2048 | bytes 520 | tf_op jit(solution)/shard_map/scatter-add | solution.py:136
  319.0 29.5 %psum.67 = f32[128]{0:T(128)S(1)} all-reduce(f32[128]{0:T(128)S(1)} %slice.370), channel_id=1, replica_groups=mesh['parts'=2,'warp'=4,'weft'=2,'ply'=2] {'warp','weft','ply'}, use_global_device_ids=true, to_apply=%region_14.15 | all-reduce | flops 128 | bytes 1024 | tf_op jit(solution)/shard_map/psum | solution.py:139
  348.8 29.5 %all-reduce.1 = f32[128]{0:T(128)S(1)} all-reduce(f32[128]{0:T(128)S(1)} %dynamic-update-slice.1), channel_id=1, replica_groups=mesh['parts'=2,'warp'=4,'weft'=2,'ply'=2] {'warp','weft','ply'}, use_global_device_ids=true, to_apply=%add.1 | all-reduce | flops 128 | bytes 1024
  378.3 12.6 %gather_fusion.9 = f32[2048]{0:T(1024)S(1)} fusion(f32[128]{0:T(128)S(1)} %all-reduce.1, s32[2048]{0:T(1024)S(1)} %broadcast_clamp_fusion), kind=kCustom, calls=%fused_computation.9 | custom fusion | bytes 24576 | tf_op jit(solution)/shard_map/gather | solution.py:146
  391.0 2.3 gather_fusion.7
  393.3 8.7 %ragged-dot-none.2 = f32[512,512]{1,0:T(8,128)} custom-call(s32[1]{0:T(128)} %get-tuple-element.27, s32[4]{0:T(128)} %get-tuple-element.28, s32[4]{0:T(128)} %get-tuple-element.29, s32[4]{0:T(128)} %get-tuple-element.30, s32[1]{0:T(128)} %get-tuple-element.27, f32[512,512]{1,0:T(8,128)} %gather_fusion.7, f32[3,512,512]{2,1,0:T(8,128)} %param.16), custom_call_target="tpu_custom_call" | custom-call | flops 268435456 | bytes 5242892 | tf_op jit(solution)/shard_map/ragged_dot_general/ragged-dot-none
  402.0 3.9 gather_fusion.8
  416.1 4.1 collective-permute-done.15
  422.3 32.2 %psum.68 = f32[]{:T(128)} all-reduce(f32[]{:T(128)} %fusion.22), channel_id=1, replica_groups=mesh['parts'=2,'warp'=4,'weft'=2,'ply'=2] {'warp','weft','ply'}, use_global_device_ids=true, to_apply=%region_16.17 | all-reduce | flops 1 | bytes 8 | tf_op jit(solution)/shard_map/psum | solution.py:151
  455.9 3.4 fusion.11
  459.2 2.3 gather_fusion.10
  461.6 8.7 %ragged-dot-none.1 = f32[512,512]{1,0:T(8,128)} custom-call(s32[1]{0:T(128)} %get-tuple-element.27, s32[4]{0:T(128)} %get-tuple-element.28, s32[4]{0:T(128)} %get-tuple-element.29, s32[4]{0:T(128)} %get-tuple-element.30, s32[1]{0:T(128)} %get-tuple-element.27, f32[512,512]{1,0:T(8,128)} %gather_fusion.10, f32[3,512,512]{2,1,0:T(8,128)} %param.17), custom_call_target="tpu_custom_call" | custom-call | flops 268435456 | bytes 5242892 | tf_op jit(solution)/shard_map/ragged_dot_general/ragged-dot-none
  470.3 3.2 gather_fusion.11
  483.1 3.1 collective-permute-done.19
  488.3 30.6 %psum.69 = f32[]{:T(128)} all-reduce(f32[]{:T(128)} %multiply_reduce_fusion), channel_id=1, replica_groups=mesh['parts'=2,'warp'=4,'weft'=2,'ply'=2] {'warp','weft','ply'}, use_global_device_ids=true, to_apply=%region_18.19 | all-reduce | flops 1 | bytes 8 | tf_op jit(solution)/shard_map/psum | solution.py:130
  522.9 14.7 %scatter_custom_fusion.2 = f32[129]{0:T(256)S(1)} fusion(s32[2048]{0:T(1024)S(1)} %bitcast.140, f32[2048]{0:T(1024)S(1)} %bitcast.141, f32[]{:T(128)} %constant.17.clone.1), kind=kCustom, calls=%fused_computation.183 | custom fusion | flops 2048 | bytes 520 | tf_op jit(solution)/shard_map/scatter-add | solution.py:136
  537.5 29.5 %psum.70 = f32[128]{0:T(128)S(1)} all-reduce(f32[128]{0:T(128)S(1)} %slice.403), channel_id=1, replica_groups=mesh['parts'=2,'warp'=4,'weft'=2,'ply'=2] {'warp','weft','ply'}, use_global_device_ids=true, to_apply=%region_21.22 | all-reduce | flops 128 | bytes 1024 | tf_op jit(solution)/shard_map/psum | solution.py:139
  567.4 29.5 %all-reduce.2 = f32[128]{0:T(128)S(1)} all-reduce(f32[128]{0:T(128)S(1)} %dynamic-update-slice.2), channel_id=1, replica_groups=mesh['parts'=2,'warp'=4,'weft'=2,'ply'=2] {'warp','weft','ply'}, use_global_device_ids=true, to_apply=%add.2 | all-reduce | flops 128 | bytes 1024
  596.8 12.6 %gather_fusion.14 = f32[2048]{0:T(1024)S(1)} fusion(f32[128]{0:T(128)S(1)} %all-reduce.2, s32[2048]{0:T(1024)S(1)} %broadcast_clamp_fusion), kind=kCustom, calls=%fused_computation.14 | custom fusion | bytes 24576 | tf_op jit(solution)/shard_map/gather | solution.py:146
  609.5 2.3 gather_fusion.12
  611.8 8.8 %ragged-dot-none = f32[512,512]{1,0:T(8,128)} custom-call(s32[1]{0:T(128)} %get-tuple-element.27, s32[4]{0:T(128)} %get-tuple-element.28, s32[4]{0:T(128)} %get-tuple-element.29, s32[4]{0:T(128)} %get-tuple-element.30, s32[1]{0:T(128)} %get-tuple-element.27, f32[512,512]{1,0:T(8,128)} %gather_fusion.12, f32[3,512,512]{2,1,0:T(8,128)} %param.16), custom_call_target="tpu_custom_call" | custom-call | flops 268435456 | bytes 5242892 | tf_op jit(solution)/shard_map/ragged_dot_general/ragged-dot-none
  620.6 3.9 gather_fusion.13
  634.8 4.1 collective-permute-done.23
  641.1 32.1 %psum.71 = f32[]{:T(128)} all-reduce(f32[]{:T(128)} %fusion.21), channel_id=1, replica_groups=mesh['parts'=2,'warp'=4,'weft'=2,'ply'=2] {'warp','weft','ply'}, use_global_device_ids=true, to_apply=%region_23.24 | all-reduce | flops 1 | bytes 8 | tf_op jit(solution)/shard_map/psum | solution.py:151
  674.4 2.7 multiply_subtract_fusion
  (256 shorter events, 87.2 us)
Async XLA Ops:
  0.6 85.5 %copy-start = (f32[3,4,512]{2,1,0:T(4,128)S(1)}, f32[3,4,512]{2,1,0:T(4,128)}, u32[]{:S(2)}) copy-start(f32[3,4,512]{2,1,0:T(4,128)} %param.18) | copy-start | bytes 73732
  11.8 408.7 %copy-start.2 = (f32[4,128,128]{2,1,0:T(8,128)}, f32[4,128,128]{2,1,0:T(8,128)S(1)}, u32[]{:S(2)}) copy-start(f32[4,128,128]{2,1,0:T(8,128)S(1)} %broadcast_in_dim.140) | copy-start | bytes 786436
  11.9 408.6 %copy-start.5 = (f32[4,128,128]{2,1,0:T(8,128)}, f32[4,128,128]{2,1,0:T(8,128)S(1)}, u32[]{:S(2)}) copy-start(f32[4,128,128]{2,1,0:T(8,128)S(1)} %broadcast_in_dim.135) | copy-start | bytes 786436
  12.0 408.5 %copy-start.8 = (f32[4,128,128]{2,1,0:T(8,128)}, f32[4,128,128]{2,1,0:T(8,128)S(1)}, u32[]{:S(2)}) copy-start(f32[4,128,128]{2,1,0:T(8,128)S(1)} %broadcast_in_dim.138) | copy-start | bytes 786436
  24.6 9.3 %copy-start.41 = (s32[4,4,128]{2,1,0:T(4,128)S(1)}, s32[4,4,128]{2,1,0:T(4,128)}, u32[]{:S(2)}) copy-start(s32[4,4,128]{2,1,0:T(4,128)} %param.15) | copy-start | bytes 24580
  27.8 7.7 %copy-start.43 = (s32[4,128]{1,0:T(4,128)S(1)}, s32[4,128]{1,0:T(4,128)}, u32[]{:S(2)}) copy-start(s32[4,128]{1,0:T(4,128)} %param.14) | copy-start | bytes 6148
  27.9 16.0 %copy-start.44 = (u32[32]{0:T(128)S(1)}, u32[32]{0:T(128)}, u32[]{:S(2)}) copy-start(u32[32]{0:T(128)} %constant.48) | copy-start | bytes 388
  29.4 19.4 %copy-start.11 = (f32[4,128,512]{2,1,0:T(8,128)S(1)}, f32[4,128,512]{2,1,0:T(8,128)}, u32[]{:S(2)}) copy-start(f32[4,128,512]{2,1,0:T(8,128)} %param.11) | copy-start | bytes 3145732
  29.4 6.2 collective-permute-start
  32.6 5.1 collective-permute-start.1
  38.5 7.7 %collective-permute-start.2 = (f32[6,1,256]{2,1,0:T(1,128)S(1)}, f32[6,1,256]{2,1,0:T(1,128)S(1)}, u32[]{:S(2)}, u32[]{:S(2)}) collective-permute-start(f32[6,1,256]{2,1,0:T(1,128)S(1)} %get-tuple-element.103), channel_id=1, source_target_pairs={{0,2},{1,3},{4,6},{5,7},{8,10},{9,11},{12,14},{13,15},{16,18},{17,... | collective-permute-start | bytes 18440 | tf_op jit(solution)/shard_map/ppermute | solution.py:19
  41.9 5.5 collective-permute-start.3
  48.8 35.8 %copy-start.39 = (f32[4,128,512]{2,1,0:T(8,128)S(1)}, f32[4,128,512]{2,1,0:T(8,128)}, u32[]{:S(2)}) copy-start(f32[4,128,512]{2,1,0:T(8,128)} %param.12) | copy-start | bytes 3145732
  49.8 81.5 %copy-start.42 = (f32[8,128]{1,0:T(8,128)S(1)}, f32[8,128]{1,0:T(8,128)}, u32[]{:S(2)}) copy-start(f32[8,128]{1,0:T(8,128)} %param.19) | copy-start | bytes 12292
  191.2 3.1 collective-permute-start.4
  193.0 3.2 collective-permute-start.5
  196.3 2.8 collective-permute-start.6
  197.6 5.5 collective-permute-start.7
  203.3 36.7 %copy-start.16 = (f32[4,128,128]{2,1,0:T(8,128)}, f32[4,128,128]{2,1,0:T(8,128)S(1)}, u32[]{:S(2)}) copy-start(f32[4,128,128]{2,1,0:T(8,128)S(1)} %get-tuple-element.73) | copy-start | bytes 786436
  255.1 8.6 %copy-start.12 = (f32[512,512]{1,0:T(8,128)S(1)}, f32[512,512]{1,0:T(8,128)}, u32[]{:S(2)}) copy-start(f32[512,512]{1,0:T(8,128)} %gather_fusion.6) | copy-start | bytes 3145732
  256.5 3.7 collective-permute-start.8
  257.8 3.2 collective-permute-start.9
  261.1 2.7 collective-permute-start.10
  262.4 5.5 collective-permute-start.11
  408.4 3.1 collective-permute-start.12
  410.2 3.2 collective-permute-start.13
  413.5 2.7 collective-permute-start.14
  414.8 5.5 collective-permute-start.15
  420.5 34.0 %copy-start.35 = (f32[4,128,128]{2,1,0:T(8,128)}, f32[4,128,128]{2,1,0:T(8,128)S(1)}, u32[]{:S(2)}) copy-start(f32[4,128,128]{2,1,0:T(8,128)S(1)} %get-tuple-element.53) | copy-start | bytes 786436
  474.6 11.7 %copy-start.14 = (f32[512,512]{1,0:T(8,128)S(1)}, f32[512,512]{1,0:T(8,128)}, u32[]{:S(2)}) copy-start(f32[512,512]{1,0:T(8,128)} %copy-done.13) | copy-start | bytes 3145732
  474.6 12.8 %copy-start.3 = (f32[4,128,128]{2,1,0:T(8,128)S(1)}, f32[4,128,128]{2,1,0:T(8,128)}, u32[]{:S(2)}) copy-start(f32[4,128,128]{2,1,0:T(8,128)} %copy-done.2) | copy-start | bytes 786436
  474.6 12.7 %copy-start.6 = (f32[4,128,128]{2,1,0:T(8,128)S(1)}, f32[4,128,128]{2,1,0:T(8,128)}, u32[]{:S(2)}) copy-start(f32[4,128,128]{2,1,0:T(8,128)} %copy-done.5) | copy-start | bytes 786436
  474.6 12.7 %copy-start.9 = (f32[4,128,128]{2,1,0:T(8,128)S(1)}, f32[4,128,128]{2,1,0:T(8,128)}, u32[]{:S(2)}) copy-start(f32[4,128,128]{2,1,0:T(8,128)} %copy-done.8) | copy-start | bytes 786436
  474.6 12.7 %copy-start.15 = (f32[4,128,512]{2,1,0:T(8,128)S(1)}, f32[4,128,512]{2,1,0:T(8,128)}, u32[]{:S(2)}) copy-start(f32[4,128,512]{2,1,0:T(8,128)} %get-tuple-element.32) | copy-start | bytes 3145732
  474.6 3.9 collective-permute-start.16
  476.2 3.2 collective-permute-start.17
  479.4 3.7 collective-permute-start.18
  480.7 5.5 collective-permute-start.19
  486.5 32.4 %copy-start.27 = (f32[4,128,128]{2,1,0:T(8,128)}, f32[4,128,128]{2,1,0:T(8,128)S(1)}, u32[]{:S(2)}) copy-start(f32[4,128,128]{2,1,0:T(8,128)S(1)} %get-tuple-element.43) | copy-start | bytes 786436
  521.8 155.4 %copy-start.1 = (f32[4,128,512]{2,1,0:T(8,128)}, f32[4,128,512]{2,1,0:T(8,128)S(1)}, u32[]{:S(2)}) copy-start(f32[4,128,512]{2,1,0:T(8,128)S(1)} %multiply_add_fusion.1) | copy-start | bytes 3145732
  626.9 13.2 %copy-start.4 = (f32[4,128,128]{2,1,0:T(8,128)S(1)}, f32[4,128,128]{2,1,0:T(8,128)}, u32[]{:S(2)}) copy-start(f32[4,128,128]{2,1,0:T(8,128)} %copy-done.2) | copy-start | bytes 786436
  627.0 13.2 %copy-start.7 = (f32[4,128,128]{2,1,0:T(8,128)S(1)}, f32[4,128,128]{2,1,0:T(8,128)}, u32[]{:S(2)}) copy-start(f32[4,128,128]{2,1,0:T(8,128)} %copy-done.5) | copy-start | bytes 786436
  627.0 13.2 %copy-start.10 = (f32[4,128,128]{2,1,0:T(8,128)S(1)}, f32[4,128,128]{2,1,0:T(8,128)}, u32[]{:S(2)}) copy-start(f32[4,128,128]{2,1,0:T(8,128)} %copy-done.8) | copy-start | bytes 786436
  627.0 3.3 collective-permute-start.20
  628.9 3.2 collective-permute-start.21
  632.1 2.7 collective-permute-start.22
  633.4 5.5 collective-permute-start.23
  674.4 2.8 copy-start.40
  (21 other events, 17.3 us)
where the time goes:
time: 681 us; the launch traced here: 679 us
  blocking collectives  368 us (54%)
  local copies, waits for them, and re-layouts  88.5 us (13%)
  other arithmetic  80.7 us (12%)
  Pallas kernels  53.8 us (8%)
  starting transfers between devices  37 us (5%)
  waiting for transfers between devices  30.1 us (4%)
  matrix products  10.3 us (2%)
  between operations  10.3 us (2%)
    psum x3, blocking collectives, on_device(): lax.psum(jnp.sum(edge_weight * direction * applied), ('warp', 'weft', 'pl...  96.3 us
    psum x3, blocking collectives, on_device(): lax.psum(jnp.sum(edge_weight * residual * precond), ('warp', 'weft', 'ply'))  94.8 us
    psum x3, blocking collectives, on_device(): coarse_rhs = lax.psum(partial_rhs, ('warp', 'weft', 'ply'))  88.5 us
    unnamed x3, blocking collectives  88.4 us
    another operation x6, Pallas kernels  52.5 us
    scatter-add x3, other arithmetic, on_device(): jax.ops.segment_sum(corner_load.reshape(-1), corner_slot.reshape(-1), num...  44 us
    gather x6, local copies, waits for them, and re-layouts, on_device(): corner_vals = jnp.where(corner_live, coarse_sol[corner_pick], 0.0)  37.9 us
    ppermute x12, waiting for transfers between devices, with_halo(): after = lax.ppermute(leading, axis, down)  30.1 us
  transfers between devices with their start and end apart: 24, of which 12 were waited for; matrix products, arithmetic and copies ran while one was open for 1% of the time, Pallas kernels for 0%

commit v1 on v0

v1 whole, which is shorter than its diff:
```python
import functools

import jax
import jax.numpy as jnp
from jax import lax
from jax.experimental import pallas as pl
from jax.experimental.pallas import tpu as pltpu
from jax.sharding import PartitionSpec as P

ITERS = 3
HIGHEST = lax.Precision.HIGHEST
F32 = jnp.float32
BF16 = jnp.bfloat16
MESH = pl.DeviceIdType.MESH
NN = (((1,), (0,)), ((), ()))
NT = (((1,), (1,)), ((), ()))
TN = (((0,), (0,)), ((), ()))


def dot(a, b, dims=NN):
    return lax.dot_general(a, b, dims, preferred_element_type=F32)


def split2(x):
    hi = x.astype(BF16)
    return hi, (x - hi.astype(F32)).astype(BF16)


def split3(x):
    hi = x.astype(BF16).astype(F32)
    rest = x - hi
    mid = rest.astype(BF16).astype(F32)
    return hi, mid, rest - mid


def kernel(
    nw, nf, npl, rows, cols, edge, npat, ncoarse,
    lam_in, res_in, dir_in, rz_in, pat, cor, sinv, sdir, shp, cinv,
    lam, res, dirn,
    m_hi, m_lo, x_hi, x_lo, masks, field, info, infosend, oht, sel, shape_f, shape_st,
    ginv, rz_slots, cv_slots, co_slots, rzprev,
    hns_send, hns_recv, hew_send, hew_recv,
    h_ssem, h_rsem, i_ssem, i_rsem, a_ssem, a_rsem,
):
    n = nw * nf * npl
    cells = rows * cols
    dof = 4 * edge
    warp, weft, ply = lax.axis_index("warp"), lax.axis_index("weft"), lax.axis_index("ply")
    me = (warp * nf + weft) * npl + ply
    tile = warp * npl + ply
    ntile = nw * npl
    has_n, has_s = tile < ntile - 1, tile > 0
    has_e, has_w = weft < nf - 1, weft > 0
    north = {"warp": (tile + 1) // npl, "ply": (tile + 1) % npl, "weft": weft}
    south = {"warp": (tile + ntile - 1) // npl % nw, "ply": (tile + npl - 1) % npl, "weft": weft}
    east = {"warp": warp, "ply": ply, "weft": weft + 1}
    west = {"warp": warp, "ply": ply, "weft": weft - 1}

    def peer(t):
        other = lax.rem(me + t, n)
        return {"warp": other // (nf * npl), "weft": other // npl % nf, "ply": other % npl}

    B_S, B_N, B_W, B_E = (cells + k * cols for k in range(4))

    for k in range(4):
        for i in range(rows):
            info[k : k + 1, i * cols : (i + 1) * cols] = cor[k, i : i + 1, :].astype(F32)
    for i in range(rows):
        info[4:5, i * cols : (i + 1) * cols] = pat[i : i + 1, :].astype(F32)
    info[5:8, 0:cells] = jnp.zeros((3, cells), F32)
    for there, lane in ((has_s, B_S), (has_n, B_N), (has_w, B_W), (has_e, B_E)):
        @pl.when(jnp.logical_not(there))
        def _():
            info[:, lane : lane + cols] = jnp.full((8, cols), -1.0, F32)
    for there, k in ((has_s, 0), (has_n, 1)):
        @pl.when(jnp.logical_not(there))
        def _():
            hns_recv[:, k] = jnp.zeros((2 * ITERS, cols, edge), F32)
    for there, k in ((has_w, 0), (has_e, 1)):
        @pl.when(jnp.logical_not(there))
        def _():
            hew_recv[:, k] = jnp.zeros((2 * ITERS, 8, edge), F32)
    own = info[:, 0:cells]
    infosend[0] = own[:, (rows - 1) * cols :]
    infosend[1] = own[:, :cols]
    cell_i = lax.broadcasted_iota(jnp.int32, (cells, cols), 0)
    lane_i = lax.broadcasted_iota(jnp.int32, (cells, cols), 1)
    for slot, j in ((2, cols - 1), (3, 0)):
        pick = jnp.where(cell_i == lane_i * cols + j, 1.0, 0.0).astype(F32)
        infosend[slot] = lax.dot_general(
            own, pick, NN, precision=HIGHEST, preferred_element_type=F32
        )
    ginv[me] = cinv[...]

    barrier = pltpu.get_barrier_semaphore()

    def greet(t, c):
        pl.semaphore_signal(barrier, inc=1, device_id=peer(t), device_id_type=MESH)
        return c

    lax.fori_loop(1, n, greet, 0)
    pl.semaphore_wait(barrier, n - 1)

    def send_all(ref, src, which):
        def one(t, c):
            pltpu.make_async_remote_copy(
                src_ref=src, dst_ref=src, send_sem=a_ssem.at[which], recv_sem=a_rsem.at[which],
                device_id=peer(t), device_id_type=MESH,
            ).start()
            return c

        lax.fori_loop(1, n, one, 0)

    def wait_all(ref, sem):
        pltpu.make_async_copy(ref, ref, sem).wait()

    send_all(None, ginv.at[me], 3 * ITERS)

    def put(src, dst, ssem, rsem, to):
        return pltpu.make_async_remote_copy(
            src_ref=src, dst_ref=dst, send_sem=ssem, recv_sem=rsem,
            device_id=to, device_id_type=MESH,
        )

    def info_copies():
        return (
            (has_n, has_s, put(infosend.at[0], info.at[:, B_S : B_S + cols], i_ssem.at[0], i_rsem.at[0], north)),
            (has_s, has_n, put(infosend.at[1], info.at[:, B_N : B_N + cols], i_ssem.at[1], i_rsem.at[1], south)),
            (has_e, has_w, put(infosend.at[2], info.at[:, B_W : B_W + cols], i_ssem.at[2], i_rsem.at[2], east)),
            (has_w, has_e, put(infosend.at[3], info.at[:, B_E : B_E + cols], i_ssem.at[3], i_rsem.at[3], west)),
        )

    def halo_copies(ph):
        return (
            (has_n, has_s, put(hns_send.at[ph, 0], hns_recv.at[ph, 0], h_ssem.at[ph, 0], h_rsem.at[ph, 0], north)),
            (has_s, has_n, put(hns_send.at[ph, 1], hns_recv.at[ph, 1], h_ssem.at[ph, 1], h_rsem.at[ph, 1], south)),
            (has_e, has_w, put(hew_send.at[ph, 0], hew_recv.at[ph, 0], h_ssem.at[ph, 2], h_rsem.at[ph, 2], east)),
            (has_w, has_e, put(hew_send.at[ph, 1], hew_recv.at[ph, 1], h_ssem.at[ph, 3], h_rsem.at[ph, 3], west)),
        )

    def start_copies(copies):
        for out, _, copy in copies:
            @pl.when(out)
            def _(copy=copy):
                copy.start()

    def wait_recv(copies):
        for _, came, copy in copies:
            @pl.when(came)
            def _(copy=copy):
                copy.wait_recv()

    def wait_send(copies):
        for out, _, copy in copies:
            @pl.when(out)
            def _(copy=copy):
                copy.wait_send()

    start_copies(info_copies())

    for src, which in ((sdir, 0), (sinv, 1)):
        for p in range(npat):
            hi, lo = split2(src[p])
            m_hi[which, p * dof : (p + 1) * dof, :] = hi
            m_lo[which, p * dof : (p + 1) * dof, :] = lo
    prow = lax.broadcasted_iota(jnp.int32, (8, cells), 0).astype(F32)
    onehot = jnp.where(prow == own[4:5, :], 1.0, 0.0).astype(F32)
    for p in range(npat):
        spread_p = jnp.where(lax.broadcasted_iota(jnp.int32, (8, edge), 0) == p, 1.0, 0.0)
        masks[p] = dot(onehot.astype(BF16), spread_p.astype(BF16), TN).astype(BF16)
    shape_f[...] = jnp.zeros_like(shape_f)
    for p in range(npat):
        shape_f[4 * p : 4 * p + 4, :] = shp[p]
    s_hi, s_lo = split2(shape_f[...])
    shape_st[0:16, :] = s_hi
    shape_st[16:32, :] = s_hi
    shape_st[32:48, :] = s_lo
    lam[...] = lam_in[...]
    res[...] = res_in[...]
    dirn[...] = dir_in[...]
    rzprev[...] = jnp.broadcast_to(rz_in[...], rzprev.shape)

    wait_recv(info_copies())
    ext = cells + 4 * cols
    row_k = lax.broadcasted_iota(jnp.int32, (16, ext), 0)
    sel[...] = jnp.where((row_k // 4).astype(F32) == info[4:5, :], 1.0, 0.0)
    coarse_row = lax.broadcasted_iota(jnp.int32, (ncoarse, ext), 0).astype(F32)
    for k in range(4):
        oht[k] = jnp.where(coarse_row == info[k : k + 1, :], 1.0, 0.0).astype(BF16)

    sub = lax.broadcasted_iota(jnp.int32, (cols, edge), 0)
    first, final = sub == 0, sub == cols - 1
    w_east = jnp.where(final & jnp.logical_not(has_e), 1.0, 0.5)
    no_w = first & jnp.logical_not(has_w)
    w_north = jnp.where(has_n, 0.5, 1.0)
    keep_s = jnp.where(has_s, 1.0, 0.0)
    BW, BE, BS, BN = (slice(b * edge, (b + 1) * edge) for b in range(4))

    def rowslice(i):
        return slice(i * cols, (i + 1) * cols)

    def set_operand(i, b, x):
        hi, lo = split2(x)
        for p in range(npat):
            m = masks[p, rowslice(i), :]
            x_hi[rowslice(i), p * dof + b * edge : p * dof + (b + 1) * edge] = hi * m
            x_lo[rowslice(i), p * dof + b * edge : p * dof + (b + 1) * edge] = lo * m

    def product(which):
        xh = x_hi[...]
        return dot(xh, m_hi[which]) + (dot(x_lo[...], m_hi[which]) + dot(xh, m_lo[which]))

    def send_halo(ph):
        hns_send[ph, 0] = field[rowslice(rows - 1), BN]
        hns_send[ph, 1] = field[rowslice(0), BS]
        for i in range(rows):
            hew_send[ph, 0, i : i + 1, :] = field[(i + 1) * cols - 1 : (i + 1) * cols, BE]
            hew_send[ph, 1, i : i + 1, :] = field[i * cols : i * cols + 1, BW]
        start_copies(halo_copies(ph))

    def fold(x):
        return jnp.sum(x.reshape(-1, 8, x.shape[-1]), axis=0)

    def lanes(x):
        total = x[:, :edge]
        for b in range(1, x.shape[1] // edge):
            total = total + x[:, b * edge : (b + 1) * edge]
        return total

    def jump(i, b, hs, hn, hw, he):
        r = rowslice(i)
        if b == 0:
            other = jnp.where(first, hw[i : i + 1, :], pltpu.roll(field[r, BE], 1, 0))
            return jnp.where(no_w, 0.0, field[r, BW] - other)
        if b == 1:
            other = jnp.where(final, he[i : i + 1, :], pltpu.roll(field[r, BW], cols - 1, 0))
            return field[r, BE] - other
        if b == 2:
            if i == 0:
                return (field[r, BS] - hs) * keep_s
            return field[r, BS] - field[rowslice(i - 1), BN]
        if i == rows - 1:
            return field[r, BN] - hn
        return field[r, BN] - field[rowslice(i + 1), BS]

    def weight(i, b):
        if b == 1:
            return w_east
        if b == 3 and i == rows - 1:
            return w_north
        return 0.5

    def total(ref):
        return jnp.sum(ref, axis=(0, 1, 2), keepdims=False)

    def everywhere(slots):
        part = jnp.sum(slots, axis=0)
        return jnp.sum(jnp.sum(part, axis=1, keepdims=True), axis=0, keepdims=True)

    rk = lax.broadcasted_iota(jnp.int32, (16, ext), 0) % 4
    rk_c = lax.broadcasted_iota(jnp.int32, (16, ncoarse), 0) % 4

    def body(it, carry):
        pa, pb = 2 * it, 2 * it + 1
        for i in range(rows):
            for b in range(4):
                set_operand(i, b, weight(i, b) * res[rowslice(i), b * edge : (b + 1) * edge])
        field[...] = product(0)
        send_halo(pa)
        acc = jnp.zeros((8, edge), F32)
        for i in range(rows):
            for b in range(4):
                bs = slice(b * edge, (b + 1) * edge)
                acc = acc + fold(weight(i, b) * res[rowslice(i), bs] * field[rowslice(i), bs])
        rz_slots[it, me] = acc
        send_all(None, rz_slots.at[it, me], 3 * it)
        wait_recv(halo_copies(pa))
        wait_all(rz_slots.at[it, pl.ds(0, n - 1)], a_rsem.at[3 * it])
        rz_now = everywhere(rz_slots[it])
        beta = rz_now / rzprev[0:1, 0:1]
        hs, hn = hns_recv[pa, 0], hns_recv[pa, 1]
        hw, he = hew_recv[pa, 0], hew_recv[pa, 1]
        for i in range(rows):
            for b in range(4):
                bs = slice(b * edge, (b + 1) * edge)
                d = weight(i, b) * jump(i, b, hs, hn, hw, he) + beta * dirn[rowslice(i), bs]
                dirn[rowslice(i), bs] = d
                set_operand(i, b, d)
        d_hi, d_lo = split2(dirn[...])
        terms = dot(s_hi, d_hi, NT) + (dot(s_lo, d_hi, NT) + dot(s_hi, d_lo, NT))
        terms = terms * sel[:, 0:cells]
        stack = jnp.concatenate(split3(terms), axis=0).astype(BF16)
        load = jnp.zeros((16, ncoarse), F32)
        for k in range(4):
            r = dot(stack, oht[k, :, 0:cells], NT)
            load = load + jnp.where(rk_c == k, r[0:16] + r[16:32] + r[32:48], 0.0)
        co_slots[it, me] = load[0:8] + load[8:16]
        send_all(None, co_slots.at[it, me], 3 * it + 1)
        field[...] = product(1)
        send_halo(pb)
        cv_slots[it, me] = lanes(fold(dirn[...] * field[...]))
        send_all(None, cv_slots.at[it, me], 3 * it + 2)

        @pl.when(it == 0)
        def _():
            wait_all(ginv.at[pl.ds(0, n - 1)], a_rsem.at[3 * ITERS])

        wait_all(co_slots.at[it, pl.ds(0, n - 1)], a_rsem.at[3 * it + 1])
        rhs = jnp.sum(jnp.sum(co_slots[it], axis=0), axis=0, keepdims=True)
        rhs = jnp.broadcast_to(rhs, (8, ncoarse))
        sol = lax.dot_general(
            rhs, ginv[...].reshape(ncoarse, ncoarse), NT, precision=HIGHEST,
            preferred_element_type=F32,
        )
        hi, mid, lo = split3(sol)
        srow = lax.broadcasted_iota(jnp.int32, (8, ncoarse), 0)
        lhs = jnp.where(srow == 0, hi, jnp.where(srow == 1, mid, jnp.where(srow == 2, lo, 0.0)))
        lhs = jnp.concatenate([lhs, jnp.zeros_like(lhs)], axis=0).astype(BF16)
        vals = jnp.zeros((16, ext), F32)
        for k in range(4):
            cv = jnp.sum(dot(lhs, oht[k]), axis=0, keepdims=True)
            vals = jnp.where(rk == k, cv, vals)
        a_hi, a_lo = split2(vals * sel[...])
        a_st = jnp.concatenate([a_hi, a_lo, a_hi], axis=0)
        field[...] = field[...] + dot(a_st[:, 0:cells], shape_st[...], TN)
        add_s = dot(a_st[:, B_S : B_S + cols], shape_st[:, BN], TN)
        add_n = dot(a_st[:, B_N : B_N + cols], shape_st[:, BS], TN)
        add_w = dot(a_st[:, B_W : B_W + cols], shape_st[:, BE], TN)
        add_e = dot(a_st[:, B_E : B_E + cols], shape_st[:, BW], TN)
        wait_recv(halo_copies(pb))
        hs, hn = hns_recv[pb, 0] + add_s, hns_recv[pb, 1] + add_n
        hw, he = hew_recv[pb, 0] + add_w[0:8], hew_recv[pb, 1] + add_e[0:8]
        wait_all(cv_slots.at[it, pl.ds(0, n - 1)], a_rsem.at[3 * it + 2])
        curvature = everywhere(cv_slots[it]) + jnp.sum(
            sol[0:1] * rhs[0:1], axis=1, keepdims=True
        )
        alpha = rz_now / curvature
        for i in range(rows):
            for b in range(4):
                bs = slice(b * edge, (b + 1) * edge)
                rs = rowslice(i)
                lam[rs, bs] = lam[rs, bs] + alpha * dirn[rs, bs]
                res[rs, bs] = res[rs, bs] - alpha * jump(i, b, hs, hn, hw, he)
        rzprev[...] = jnp.broadcast_to(rz_now, rzprev.shape)
        return carry

    lax.fori_loop(0, ITERS, body, 0)

    wait_send(info_copies())
    wait_all(ginv.at[pl.ds(0, n - 1)], a_ssem.at[3 * ITERS])
    for it in range(ITERS):
        wait_send(halo_copies(2 * it))
        wait_send(halo_copies(2 * it + 1))
        wait_all(rz_slots.at[it, pl.ds(0, n - 1)], a_ssem.at[3 * it])
        wait_all(co_slots.at[it, pl.ds(0, n - 1)], a_ssem.at[3 * it + 1])
        wait_all(cv_slots.at[it, pl.ds(0, n - 1)], a_ssem.at[3 * it + 2])


def on_device(
    lam_start, resid_start, dirn_start, rz_start, pattern, corners,
    schur_inv, schur_dirichlet, corner_shape, coarse_inv,
):
    rows, cols, dof = lam_start.shape
    edge = dof // 4
    npat = schur_inv.shape[0]
    ncoarse = coarse_inv.shape[1]
    nw, nf, npl = lax.axis_size("warp"), lax.axis_size("weft"), lax.axis_size("ply")
    n = nw * nf * npl
    cells = rows * cols
    ext = cells + 4 * cols
    vmem = pl.BlockSpec(memory_space=pltpu.VMEM)
    out = jax.ShapeDtypeStruct((cells, dof), F32)
    V = pltpu.VMEM
    D = pltpu.SemaphoreType.DMA
    outs = pl.pallas_call(
        functools.partial(kernel, nw, nf, npl, rows, cols, edge, npat, ncoarse),
        out_shape=(out, out, out),
        in_specs=[vmem] * 10,
        out_specs=(vmem, vmem, vmem),
        scratch_shapes=[
            V((2, npat * dof, dof), BF16),
            V((2, npat * dof, dof), BF16),
            V((cells, npat * dof), BF16),
            V((cells, npat * dof), BF16),
            V((npat, cells, edge), BF16),
            V((cells, dof), F32),
            V((8, ext), F32),
            V((4, 8, cols), F32),
            V((4, ncoarse, ext), BF16),
            V((16, ext), F32),
            V((16, dof), F32),
            V((48, dof), BF16),
            V((n, ncoarse // n, ncoarse), F32),
            V((ITERS, n, 8, edge), F32),
            V((ITERS, n, 8, edge), F32),
            V((ITERS, n, 8, ncoarse), F32),
            V((8, 128), F32),
            V((2 * ITERS, 2, cols, edge), F32),
            V((2 * ITERS, 2, cols, edge), F32),
            V((2 * ITERS, 2, 8, edge), F32),
            V((2 * ITERS, 2, 8, edge), F32),
            D((2 * ITERS, 4)),
            D((2 * ITERS, 4)),
            D((4,)),
            D((4,)),
            D((3 * ITERS + 1,)),
            D((3 * ITERS + 1,)),
        ],
        compiler_params=pltpu.CompilerParams(
            collective_id=0, has_side_effects=True, vmem_limit_bytes=60 * 1024 * 1024
        ),
    )(
        lam_start.reshape(cells, dof), resid_start.reshape(cells, dof),
        dirn_start.reshape(cells, dof), rz_start.reshape(1, 1), pattern, corners,
        schur_inv, schur_dirichlet, corner_shape, coarse_inv,
    )
    return tuple(o.reshape(rows, cols, dof) for o in outs)


def solution(mesh):
    field = P(("parts", "warp", "ply"), "weft", None)
    return jax.shard_map(
        on_device,
        mesh=mesh,
        in_specs=(
            field, field, field,
            P("parts"),
            P(("parts", "warp", "ply"), "weft"),
            P(None, ("parts", "warp", "ply"), "weft"),
            P(), P(), P(),
            P(("parts", "warp", "weft", "ply"), None),
        ),
        out_specs=(field, field, field),
        check_vma=False,
    )
```

time: 681 us -> 74 us (0.11)
  blocking collectives: 368 us -> 0 us
  local copies, waits for them, and re-layouts: 88.5 us -> 5.59 us
  other arithmetic: 80.7 us -> 0 us
  starting transfers between devices: 37 us -> 0 us
  waiting for transfers between devices: 30.1 us -> 0 us
  Pallas kernels: 53.8 us -> 67 us
  matrix products: 10.3 us -> 0 us
  between operations: 10.3 us -> 1.3 us
    psum x9 -> x0, blocking collectives: 280 us -> none  [the longest x3 96.3 us: on_device(): lax.psum(jnp.sum(edge_weight * direction * applied), ('warp', 'weft', 'pl...]
    unnamed x3 -> x0, blocking collectives: 88.4 us -> none
    gather x18 -> x0, local copies, waits for them, and re-layouts: 74.1 us -> none  [the longest x6 37.9 us: on_device(): corner_vals = jnp.where(corner_live, coarse_sol[corner_pick], 0.0)]
    pallas_call x0 -> x1, Pallas kernels: none -> 67 us  [on_device(): pl.pallas_call(functools.partial(kernel, nw, nf, npl, rows, cols, edge, n...]
    another operation x6 -> x0, Pallas kernels: 52.5 us -> none
    scatter-add x3 -> x0, other arithmetic: 44 us -> none  [on_device(): jax.ops.segment_sum(corner_load.reshape(-1), corner_slot.reshape(-1), num...]
    ppermute x24 -> x0, starting transfers between devices: 37 us -> none  [the longest x12 21.3 us: with_halo(): before = lax.ppermute(last, axis, up)]
    ppermute x24 -> x0, waiting for transfers between devices: 30.1 us -> none  [the longest x12 30.1 us: with_halo(): after = lax.ppermute(leading, axis, down)]
  transfers between devices with their start and end apart: 24 -> 0, of which waited for: 12 -> 0; matrix products, arithmetic and copies ran while one was open for 1% -> 0% of each run, Pallas kernels for 0% -> 0%
where the time goes in v1:
time: 74 us; the launch traced here: 73.8 us
  Pallas kernels  67 us (91%)
  local copies, waits for them, and re-layouts  5.59 us (8%)
  between operations  1.3 us (2%)
    pallas_call x1, Pallas kernels, on_device(): pl.pallas_call(functools.partial(kernel, nw, nf, npl, rows, cols, edge, n...  67 us
    unnamed x5, local copies, waits for them, and re-layouts  5.59 us

profile of v1, /device:TPU:0, one launch (start us, length us, event | category | flops | bytes accessed | tf_op | source)
XLA Modules:
  0.0 73.8 jit_solution(16101937641260892212)
XLA Ops:
  1.3 67.0 %shard_map.121 = (f32[512,512]{1,0:T(8,128)}, f32[512,512]{1,0:T(8,128)}, f32[512,512]{1,0:T(8,128)}) custom-call(f32[512,512]{1,0:T(8,128)} %bitcast.8, f32[512,512]{1,0:T(8,128)} %bitcast.9, f32[512,512]{1,0:T(8,128)} %bitcast.10, f32[1,1]{1,0:T(1,128)} %bitcast.7.rz_in, s32[4,128]{1,0:T(4,128)} %pat.1, s32[4,4,128]{2,1,0:T(4,128)} %cor.1, ...), custom_call_target="tpu_custom_call" | custom-call | tf_op jit(solution)/shard_map/pallas_call | solution.py:375
  68.2 0.0 copy-start
  68.3 2.4 %copy.17 = f32[4,128,512]{2,1,0:T(8,128)} copy(f32[4,128,512]{2,1,0:T(8,128)} %bitcast.13) | data formatting | bytes 2097152
  70.6 2.3 %copy.18 = f32[4,128,512]{2,1,0:T(8,128)} copy(f32[4,128,512]{2,1,0:T(8,128)} %bitcast.12) | data formatting | bytes 2097152
  72.9 0.0 copy-done
  72.9 1.0 %copy.19 = f32[4,128,512]{2,1,0:T(8,128)} copy(f32[4,128,512]{2,1,0:T(8,128)S(1)} %bitcast.11) | data formatting | bytes 2097152
Async XLA Ops:
  68.2 4.6 %copy-start = (f32[512,512]{1,0:T(8,128)S(1)}, f32[512,512]{1,0:T(8,128)}, u32[]{:S(2)}) copy-start(f32[512,512]{1,0:T(8,128)} %get-tuple-element.8) | copy-start | bytes 3145732

commit v2 on v1

--- a/solution.py
+++ b/solution.py
@@ -37,10 +37,11 @@
     nw, nf, npl, rows, cols, edge, npat, ncoarse,
     lam_in, res_in, dir_in, rz_in, pat, cor, sinv, sdir, shp, cinv,
     lam, res, dirn,
-    m_hi, m_lo, x_hi, x_lo, masks, field, info, infosend, oht, sel, shape_f, shape_st,
-    ginv, rz_slots, cv_slots, co_slots, rzprev,
+    sdir_v, sinv_v, s_f, p_f, f_f, app, hp_ns, hp_ew, scal, crhs,
+    m_hi, m_lo, x_hi, x_lo, masks, info, infosend, oht, sel, shape_f, shape_st,
+    ginv, rz_slots, cv_slots, co_slots,
     hns_send, hns_recv, hew_send, hew_recv,
-    h_ssem, h_rsem, i_ssem, i_rsem, a_ssem, a_rsem,
+    h_ssem, h_rsem, i_ssem, i_rsem, a_ssem, a_rsem, l_sem,
 ):
     n = nw * nf * npl
     cells = rows * cols
@@ -60,7 +61,23 @@
         other = lax.rem(me + t, n)
         return {"warp": other // (nf * npl), "weft": other // npl % nf, "ply": other % npl}
 
+    RZ, ALPHA, EARLY, LATE, CC = range(5)
     B_S, B_N, B_W, B_E = (cells + k * cols for k in range(4))
+
+    barrier = pltpu.get_barrier_semaphore()
+
+    def greet(t, c):
+        pl.semaphore_signal(barrier, inc=1, device_id=peer(t), device_id_type=MESH)
+        return c
+
+    loads = [
+        pltpu.make_async_copy(src, dst, l_sem.at[k])
+        for k, (src, dst) in enumerate(
+            ((sdir, sdir_v), (res_in, res), (dir_in, dirn), (sinv, sinv_v), (lam_in, lam))
+        )
+    ]
+    for load in loads:
+        load.start()
 
     for k in range(4):
         for i in range(rows):
@@ -91,15 +108,7 @@
             own, pick, NN, precision=HIGHEST, preferred_element_type=F32
         )
     ginv[me] = cinv[...]
-
-    barrier = pltpu.get_barrier_semaphore()
-
-    def greet(t, c):
-        pl.semaphore_signal(barrier, inc=1, device_id=peer(t), device_id_type=MESH)
-        return c
-
     lax.fori_loop(1, n, greet, 0)
-    pl.semaphore_wait(barrier, n - 1)
 
     def send_all(ref, src, which):
         def one(t, c):
@@ -114,8 +123,6 @@
     def wait_all(ref, sem):
         pltpu.make_async_copy(ref, ref, sem).wait()
 
-    send_all(None, ginv.at[me], 3 * ITERS)
-
     def put(src, dst, ssem, rsem, to):
         return pltpu.make_async_remote_copy(
             src_ref=src, dst_ref=dst, send_sem=ssem, recv_sem=rsem,
@@ -156,13 +163,12 @@
             def _(copy=copy):
                 copy.wait_send()
 
-    start_copies(info_copies())
-
-    for src, which in ((sdir, 0), (sinv, 1)):
+    def split_matrices(src, which):
         for p in range(npat):
             hi, lo = split2(src[p])
             m_hi[which, p * dof : (p + 1) * dof, :] = hi
             m_lo[which, p * dof : (p + 1) * dof, :] = lo
+
     prow = lax.broadcasted_iota(jnp.int32, (8, cells), 0).astype(F32)
     onehot = jnp.where(prow == own[4:5, :], 1.0, 0.0).astype(F32)
     for p in range(npat):
@@ -175,18 +181,17 @@
     shape_st[0:16, :] = s_hi
     shape_st[16:32, :] = s_hi
     shape_st[32:48, :] = s_lo
-    lam[...] = lam_in[...]
-    res[...] = res_in[...]
-    dirn[...] = dir_in[...]
-    rzprev[...] = jnp.broadcast_to(rz_in[...], rzprev.shape)
-
-    wait_recv(info_copies())
+    for ref in (s_f, p_f, hp_ns, hp_ew, crhs):
+        ref[...] = jnp.zeros_like(ref)
+    scal[RZ] = jnp.broadcast_to(rz_in[...], (8, edge))
     ext = cells + 4 * cols
-    row_k = lax.broadcasted_iota(jnp.int32, (16, ext), 0)
-    sel[...] = jnp.where((row_k // 4).astype(F32) == info[4:5, :], 1.0, 0.0)
-    coarse_row = lax.broadcasted_iota(jnp.int32, (ncoarse, ext), 0).astype(F32)
-    for k in range(4):
-        oht[k] = jnp.where(coarse_row == info[k : k + 1, :], 1.0, 0.0).astype(BF16)
+
+    def coarse_tables():
+        row_k = lax.broadcasted_iota(jnp.int32, (16, ext), 0)
+        sel[...] = jnp.where((row_k // 4).astype(F32) == info[4:5, :], 1.0, 0.0)
+        coarse_row = lax.broadcasted_iota(jnp.int32, (ncoarse, ext), 0).astype(F32)
+        for k in range(4):
+            oht[k] = jnp.where(coarse_row == info[k : k + 1, :], 1.0, 0.0).astype(BF16)
 
     sub = lax.broadcasted_iota(jnp.int32, (cols, edge), 0)
     first, final = sub == 0, sub == cols - 1
@@ -206,17 +211,22 @@
             x_hi[rowslice(i), p * dof + b * edge : p * dof + (b + 1) * edge] = hi * m
             x_lo[rowslice(i), p * dof + b * edge : p * dof + (b + 1) * edge] = lo * m
 
-    def product(which):
+    def product(which, half):
         xh = x_hi[...]
-        return dot(xh, m_hi[which]) + (dot(x_lo[...], m_hi[which]) + dot(xh, m_lo[which]))
-
-    def send_halo(ph):
+        hs = slice(half * 2 * edge, (half + 1) * 2 * edge)
+        mh = m_hi[which, :, hs]
+        return dot(xh, mh) + (dot(x_lo[...], mh) + dot(xh, m_lo[which, :, hs]))
+
+    def send_ns(ph, field):
         hns_send[ph, 0] = field[rowslice(rows - 1), BN]
         hns_send[ph, 1] = field[rowslice(0), BS]
+        start_copies(halo_copies(ph)[0:2])
+
+    def send_ew(ph, field):
         for i in range(rows):
             hew_send[ph, 0, i : i + 1, :] = field[(i + 1) * cols - 1 : (i + 1) * cols, BE]
             hew_send[ph, 1, i : i + 1, :] = field[i * cols : i * cols + 1, BW]
-        start_copies(halo_copies(ph))
+        start_copies(halo_copies(ph)[2:4])
 
     def fold(x):
         return jnp.sum(x.reshape(-1, 8, x.shape[-1]), axis=0)
@@ -227,7 +237,7 @@
             total = total + x[:, b * edge : (b + 1) * edge]
         return total
 
-    def jump(i, b, hs, hn, hw, he):
+    def jump(field, i, b, hs, hn, hw, he):
         r = rowslice(i)
         if b == 0:
             other = jnp.where(first, hw[i : i + 1, :], pltpu.roll(field[r, BE], 1, 0))
@@ -250,9 +260,6 @@
             return w_north
         return 0.5
 
-    def total(ref):
-        return jnp.sum(ref, axis=(0, 1, 2), keepdims=False)
-
     def everywhere(slots):
         part = jnp.sum(slots, axis=0)
         return jnp.sum(jnp.sum(part, axis=1, keepdims=True), axis=0, keepdims=True)
@@ -260,33 +267,101 @@
     rk = lax.broadcasted_iota(jnp.int32, (16, ext), 0) % 4
     rk_c = lax.broadcasted_iota(jnp.int32, (16, ncoarse), 0) % 4
 
+    def step_length(it):
+        wait_all(cv_slots.at[it, pl.ds(0, n - 1)], a_rsem.at[3 * it + 2])
+        curvature = everywhere(cv_slots[it]) + scal[CC, 0:1, 0:1]
+        scal[ALPHA] = scal[RZ] / curvature
+
+    def advance():
+        alpha = scal[ALPHA, 0:1, :]
+        for b in range(4):
+            bs = slice(b * edge, (b + 1) * edge)
+            res[:, bs] = res[:, bs] - alpha * app[:, bs]
+            lam[:, bs] = lam[:, bs] + alpha * dirn[:, bs]
+
+    def take_rz(it, which):
+        wait_all(rz_slots.at[it, pl.ds(0, n - 1)], a_rsem.at[3 * it])
+        rz_now = jnp.broadcast_to(everywhere(rz_slots[it]), (8, edge))
+        scal[which] = rz_now / scal[RZ]
+        scal[RZ] = rz_now
+
+    loads[0].wait()
+    split_matrices(sdir_v, 0)
+    loads[1].wait()
+    for i in range(rows):
+        for b in range(4):
+            set_operand(i, b, weight(i, b) * res[rowslice(i), b * edge : (b + 1) * edge])
+    pl.semaphore_wait(barrier, n - 1)
+    start_copies(info_copies())
+    send_all(None, ginv.at[me], 3 * ITERS)
+    WE, SN = slice(0, 2 * edge), slice(2 * edge, 4 * edge)
+
+    def both(x):
+        return jnp.concatenate([x, x], axis=1)
+
     def body(it, carry):
         pa, pb = 2 * it, 2 * it + 1
-        for i in range(rows):
-            for b in range(4):
-                set_operand(i, b, weight(i, b) * res[rowslice(i), b * edge : (b + 1) * edge])
-        field[...] = product(0)
-        send_halo(pa)
+        new = product(0, 1)
+
+        @pl.when(it == 0)
+        def _():
+            scal[ALPHA] = jnp.full((8, edge), -1.0, F32)
+
+        @pl.when(it > 0)
+        def _():
+            step_length(it - 1)
+
+        alpha2 = both(scal[ALPHA, 0:1, :])
+        s_f[:, SN] = s_f[:, SN] - alpha2 * new
+        send_ns(pa, s_f)
+        s_f[:, WE] = s_f[:, WE] - alpha2 * product(0, 0)
+        send_ew(pa, s_f)
+
+        @pl.when(it > 0)
+        def _():
+            advance()
+
         acc = jnp.zeros((8, edge), F32)
         for i in range(rows):
             for b in range(4):
                 bs = slice(b * edge, (b + 1) * edge)
-                acc = acc + fold(weight(i, b) * res[rowslice(i), bs] * field[rowslice(i), bs])
+                acc = acc + fold(weight(i, b) * res[rowslice(i), bs] * s_f[rowslice(i), bs])
         rz_slots[it, me] = acc
         send_all(None, rz_slots.at[it, me], 3 * it)
-        wait_recv(halo_copies(pa))
-        wait_all(rz_slots.at[it, pl.ds(0, n - 1)], a_rsem.at[3 * it])
-        rz_now = everywhere(rz_slots[it])
-        beta = rz_now / rzprev[0:1, 0:1]
+
+        @pl.when(it == 0)
+        def _():
+            loads[3].wait()
+            split_matrices(sinv_v, 1)
+            wait_recv(info_copies())
+            coarse_tables()
+            loads[2].wait()
+            loads[4].wait()
+            take_rz(it, EARLY)
+            scal[LATE] = jnp.zeros((8, edge), F32)
+
+        @pl.when(it > 0)
+        def _():
+            scal[EARLY] = jnp.zeros((8, edge), F32)
+
+        early = scal[EARLY, 0:1, :]
+
+        def towards(b, hs, hn, hw, he):
+            bs = slice(b * edge, (b + 1) * edge)
+            for i in range(rows):
+                w = weight(i, b) * jump(s_f, i, b, hs, hn, hw, he) + early * dirn[rowslice(i), bs]
+                app[rowslice(i), bs] = w
+                set_operand(i, b, w)
+
+        wait_recv(halo_copies(pa)[0:2])
         hs, hn = hns_recv[pa, 0], hns_recv[pa, 1]
+        towards(2, hs, hn, None, None)
+        towards(3, hs, hn, None, None)
+        wait_recv(halo_copies(pa)[2:4])
         hw, he = hew_recv[pa, 0], hew_recv[pa, 1]
-        for i in range(rows):
-            for b in range(4):
-                bs = slice(b * edge, (b + 1) * edge)
-                d = weight(i, b) * jump(i, b, hs, hn, hw, he) + beta * dirn[rowslice(i), bs]
-                dirn[rowslice(i), bs] = d
-                set_operand(i, b, d)
-        d_hi, d_lo = split2(dirn[...])
+        towards(0, None, None, hw, he)
+        towards(1, None, None, hw, he)
+        d_hi, d_lo = split2(app[...])
         terms = dot(s_hi, d_hi, NT) + (dot(s_lo, d_hi, NT) + dot(s_hi, d_lo, NT))
         terms = terms * sel[:, 0:cells]
         stack = jnp.concatenate(split3(terms), axis=0).astype(BF16)
@@ -296,9 +371,25 @@
             load = load + jnp.where(rk_c == k, r[0:16] + r[16:32] + r[32:48], 0.0)
         co_slots[it, me] = load[0:8] + load[8:16]
         send_all(None, co_slots.at[it, me], 3 * it + 1)
-        field[...] = product(1)
-        send_halo(pb)
-        cv_slots[it, me] = lanes(fold(dirn[...] * field[...]))
+        f_f[:, SN] = product(1, 1)
+        send_ns(pb, f_f)
+        f_f[:, WE] = product(1, 0)
+        send_ew(pb, f_f)
+
+        @pl.when(it > 0)
+        def _():
+            take_rz(it, LATE)
+
+        late = scal[LATE, 0:1, :]
+        acc = jnp.zeros((8, edge), F32)
+        for b in range(4):
+            bs = slice(b * edge, (b + 1) * edge)
+            d = app[:, bs] + late * dirn[:, bs]
+            q = f_f[:, bs] + late * p_f[:, bs]
+            dirn[:, bs] = d
+            p_f[:, bs] = q
+            acc = acc + fold(d * q)
+        cv_slots[it, me] = acc
         send_all(None, cv_slots.at[it, me], 3 * it + 2)
 
         @pl.when(it == 0)
@@ -307,11 +398,13 @@
 
         wait_all(co_slots.at[it, pl.ds(0, n - 1)], a_rsem.at[3 * it + 1])
         rhs = jnp.sum(jnp.sum(co_slots[it], axis=0), axis=0, keepdims=True)
-        rhs = jnp.broadcast_to(rhs, (8, ncoarse))
+        rhs = jnp.broadcast_to(rhs, (8, ncoarse)) + scal[LATE, :, 0:1] * crhs[...]
+        crhs[...] = rhs
         sol = lax.dot_general(
             rhs, ginv[...].reshape(ncoarse, ncoarse), NT, precision=HIGHEST,
             preferred_element_type=F32,
         )
+        scal[CC] = jnp.broadcast_to(jnp.sum(sol * rhs, axis=1, keepdims=True), (8, edge))
         hi, mid, lo = split3(sol)
         srow = lax.broadcasted_iota(jnp.int32, (8, ncoarse), 0)
         lhs = jnp.where(srow == 0, hi, jnp.where(srow == 1, mid, jnp.where(srow == 2, lo, 0.0)))
@@ -322,29 +415,28 @@
             vals = jnp.where(rk == k, cv, vals)
         a_hi, a_lo = split2(vals * sel[...])
         a_st = jnp.concatenate([a_hi, a_lo, a_hi], axis=0)
-        field[...] = field[...] + dot(a_st[:, 0:cells], shape_st[...], TN)
+        f_f[...] = p_f[...] + dot(a_st[:, 0:cells], shape_st[...], TN)
         add_s = dot(a_st[:, B_S : B_S + cols], shape_st[:, BN], TN)
         add_n = dot(a_st[:, B_N : B_N + cols], shape_st[:, BS], TN)
         add_w = dot(a_st[:, B_W : B_W + cols], shape_st[:, BE], TN)
         add_e = dot(a_st[:, B_E : B_E + cols], shape_st[:, BW], TN)
         wait_recv(halo_copies(pb))
-        hs, hn = hns_recv[pb, 0] + add_s, hns_recv[pb, 1] + add_n
-        hw, he = hew_recv[pb, 0] + add_w[0:8], hew_recv[pb, 1] + add_e[0:8]
-        wait_all(cv_slots.at[it, pl.ds(0, n - 1)], a_rsem.at[3 * it + 2])
-        curvature = everywhere(cv_slots[it]) + jnp.sum(
-            sol[0:1] * rhs[0:1], axis=1, keepdims=True
-        )
-        alpha = rz_now / curvature
+        for k in range(2):
+            hp_ns[k] = hns_recv[pb, k] + late * hp_ns[k]
+            hp_ew[k] = hew_recv[pb, k] + late * hp_ew[k]
+        hs, hn = hp_ns[0] + add_s, hp_ns[1] + add_n
+        hw, he = hp_ew[0] + add_w[0:8], hp_ew[1] + add_e[0:8]
         for i in range(rows):
             for b in range(4):
                 bs = slice(b * edge, (b + 1) * edge)
-                rs = rowslice(i)
-                lam[rs, bs] = lam[rs, bs] + alpha * dirn[rs, bs]
-                res[rs, bs] = res[rs, bs] - alpha * jump(i, b, hs, hn, hw, he)
-        rzprev[...] = jnp.broadcast_to(rz_now, rzprev.shape)
+                x = jump(f_f, i, b, hs, hn, hw, he)
+                app[rowslice(i), bs] = x
+                set_operand(i, b, weight(i, b) * x)
         return carry
 
     lax.fori_loop(0, ITERS, body, 0)
+    step_length(ITERS - 1)
+    advance()
 
     wait_send(info_copies())
     wait_all(ginv.at[pl.ds(0, n - 1)], a_ssem.at[3 * ITERS])
@@ -369,21 +461,32 @@
     cells = rows * cols
     ext = cells + 4 * cols
     vmem = pl.BlockSpec(memory_space=pltpu.VMEM)
-    out = jax.ShapeDtypeStruct((cells, dof), F32)
+    hbm = pl.BlockSpec(memory_space=pltpu.HBM)
+    out = pltpu.VMEM((cells, dof), F32)
     V = pltpu.VMEM
     D = pltpu.SemaphoreType.DMA
+    limit = 121 * 512 * 1024
     outs = pl.pallas_call(
         functools.partial(kernel, nw, nf, npl, rows, cols, edge, npat, ncoarse),
         out_shape=(out, out, out),
-        in_specs=[vmem] * 10,
+        in_specs=[hbm] * 3 + [vmem] * 3 + [hbm] * 2 + [vmem] * 2,
         out_specs=(vmem, vmem, vmem),
         scratch_shapes=[
+            V((npat, dof, dof), F32),
+            V((npat, dof, dof), F32),
+            V((cells, dof), F32),
+            V((cells, dof), F32),
+            V((cells, dof), F32),
+            V((cells, dof), F32),
+            V((2, cols, edge), F32),
+            V((2, 8, edge), F32),
+            V((5, 8, edge), F32),
+            V((8, ncoarse), F32),
             V((2, npat * dof, dof), BF16),
             V((2, npat * dof, dof), BF16),
             V((cells, npat * dof), BF16),
             V((cells, npat * dof), BF16),
             V((npat, cells, edge), BF16),
-            V((cells, dof), F32),
             V((8, ext), F32),
             V((4, 8, cols), F32),
             V((4, ncoarse, ext), BF16),
@@ -394,7 +497,6 @@
             V((ITERS, n, 8, edge), F32),
             V((ITERS, n, 8, edge), F32),
             V((ITERS, n, 8, ncoarse), F32),
-            V((8, 128), F32),
             V((2 * ITERS, 2, cols, edge), F32),
             V((2 * ITERS, 2, cols, edge), F32),
             V((2 * ITERS, 2, 8, edge), F32),
@@ -405,9 +507,10 @@
             D((4,)),
             D((3 * ITERS + 1,)),
             D((3 * ITERS + 1,)),
+            D((5,)),
         ],
         compiler_params=pltpu.CompilerParams(
-            collective_id=0, has_side_effects=True, vmem_limit_bytes=60 * 1024 * 1024
+            collective_id=0, has_side_effects=True, vmem_limit_bytes=limit
         ),
     )(
         lam_start.reshape(cells, dof), resid_start.reshape(cells, dof),

time: 74 us -> 70.1 us (0.947)
  local copies, waits for them, and re-layouts: 5.59 us -> 2.91 us
  Pallas kernels: 67 us -> 65.7 us
    unnamed x5 -> x3, local copies, waits for them, and re-layouts: 5.59 us -> 2.91 us
    pallas_call x1, Pallas kernels: 67 us -> 65.7 us  [on_device(): pl.pallas_call(functools.partial(kernel, nw, nf, npl, rows, cols, edge, n...]
where the time goes in v2:
time: 70.1 us; the launch traced here: 69.9 us
  Pallas kernels  65.7 us (94%)
  local copies, waits for them, and re-layouts  2.91 us (4%)
  between operations  1.29 us (2%)
    pallas_call x1, Pallas kernels, on_device(): pl.pallas_call(functools.partial(kernel, nw, nf, npl, rows, cols, edge, n...  65.7 us
    unnamed x3, local copies, waits for them, and re-layouts  2.91 us

profile of v2, /device:TPU:0, one launch (start us, length us, event | category | flops | bytes accessed | tf_op | source)
XLA Modules:
  0.0 69.9 jit_solution(5612084476887276323)
XLA Ops:
  1.3 65.7 %shard_map.121 = (f32[512,512]{1,0:T(8,128)S(1)}, f32[512,512]{1,0:T(8,128)S(1)}, f32[512,512]{1,0:T(8,128)S(1)}) custom-call(f32[512,512]{1,0:T(8,128)} %bitcast.11, f32[512,512]{1,0:T(8,128)} %bitcast.12, f32[512,512]{1,0:T(8,128)} %bitcast.13, f32[1,1]{1,0:T(1,128)} %bitcast.7.rz_in, s32[4,128]{1,0:T(4,128)} %pat.1, s32[4,4,128]{2,1,0:T(4,128)} %cor.1, ...), custom_call_target="tpu_custom_call" | custom-call | tf_op jit(solution)/shard_map/pallas_call | solution.py:469
  67.0 1.0 %copy.16 = f32[4,128,512]{2,1,0:T(8,128)} copy(f32[4,128,512]{2,1,0:T(8,128)S(1)} %bitcast.10) | data formatting | bytes 2097152
  67.9 1.0 %copy.17 = f32[4,128,512]{2,1,0:T(8,128)} copy(f32[4,128,512]{2,1,0:T(8,128)S(1)} %bitcast.9) | data formatting | bytes 2097152
  68.9 1.0 %copy.18 = f32[4,128,512]{2,1,0:T(8,128)} copy(f32[4,128,512]{2,1,0:T(8,128)S(1)} %bitcast.8) | data formatting | bytes 2097152

commit v3 on v2

--- a/solution.py
+++ b/solution.py
@@ -211,11 +211,10 @@
             x_hi[rowslice(i), p * dof + b * edge : p * dof + (b + 1) * edge] = hi * m
             x_lo[rowslice(i), p * dof + b * edge : p * dof + (b + 1) * edge] = lo * m
 
-    def product(which, half):
+    def product(which):
         xh = x_hi[...]
-        hs = slice(half * 2 * edge, (half + 1) * 2 * edge)
-        mh = m_hi[which, :, hs]
-        return dot(xh, mh) + (dot(x_lo[...], mh) + dot(xh, m_lo[which, :, hs]))
+        mh = m_hi[which]
+        return dot(xh, mh) + (dot(x_lo[...], mh) + dot(xh, m_lo[which]))
 
     def send_ns(ph, field):
         hns_send[ph, 0] = field[rowslice(rows - 1), BN]
@@ -301,7 +300,7 @@
 
     def body(it, carry):
         pa, pb = 2 * it, 2 * it + 1
-        new = product(0, 1)
+        new = product(0)
 
         @pl.when(it == 0)
         def _():
@@ -312,9 +311,8 @@
             step_length(it - 1)
 
         alpha2 = both(scal[ALPHA, 0:1, :])
-        s_f[:, SN] = s_f[:, SN] - alpha2 * new
+        s_f[...] = s_f[...] - both(alpha2) * new
         send_ns(pa, s_f)
-        s_f[:, WE] = s_f[:, WE] - alpha2 * product(0, 0)
         send_ew(pa, s_f)
 
         @pl.when(it > 0)
@@ -371,9 +369,8 @@
             load = load + jnp.where(rk_c == k, r[0:16] + r[16:32] + r[32:48], 0.0)
         co_slots[it, me] = load[0:8] + load[8:16]
         send_all(None, co_slots.at[it, me], 3 * it + 1)
-        f_f[:, SN] = product(1, 1)
+        f_f[...] = product(1)
         send_ns(pb, f_f)
-        f_f[:, WE] = product(1, 0)
         send_ew(pb, f_f)
 
         @pl.when(it > 0)

time: 70.1 us -> 58.8 us (0.84)
  Pallas kernels: 65.7 us -> 54.4 us
    pallas_call x1, Pallas kernels: 65.7 us -> 54.4 us  [on_device(): pl.pallas_call(functools.partial(kernel, nw, nf, npl, rows, cols, edge, n...]
where the time goes in v3:
time: 58.8 us; the launch traced here: 58.6 us
  Pallas kernels  54.4 us (93%)
  local copies, waits for them, and re-layouts  2.91 us (5%)
  between operations  1.29 us (2%)
    pallas_call x1, Pallas kernels, on_device(): pl.pallas_call(functools.partial(kernel, nw, nf, npl, rows, cols, edge, n...  54.4 us
    unnamed x3, local copies, waits for them, and re-layouts  2.91 us

profile of v3, /device:TPU:0, one launch (start us, length us, event | category | flops | bytes accessed | tf_op | source)
XLA Modules:
  0.0 58.6 jit_solution(565528472457005195)
XLA Ops:
  1.3 54.4 %shard_map.121 = (f32[512,512]{1,0:T(8,128)S(1)}, f32[512,512]{1,0:T(8,128)S(1)}, f32[512,512]{1,0:T(8,128)S(1)}) custom-call(f32[512,512]{1,0:T(8,128)} %bitcast.11, f32[512,512]{1,0:T(8,128)} %bitcast.12, f32[512,512]{1,0:T(8,128)} %bitcast.13, f32[1,1]{1,0:T(1,128)} %bitcast.7.rz_in, s32[4,128]{1,0:T(4,128)} %pat.1, s32[4,4,128]{2,1,0:T(4,128)} %cor.1, ...), custom_call_target="tpu_custom_call" | custom-call | tf_op jit(solution)/shard_map/pallas_call | solution.py:466
  55.7 1.0 %copy.16 = f32[4,128,512]{2,1,0:T(8,128)} copy(f32[4,128,512]{2,1,0:T(8,128)S(1)} %bitcast.10) | data formatting | bytes 2097152
  56.7 1.0 %copy.17 = f32[4,128,512]{2,1,0:T(8,128)} copy(f32[4,128,512]{2,1,0:T(8,128)S(1)} %bitcast.9) | data formatting | bytes 2097152
  57.7 1.0 %copy.18 = f32[4,128,512]{2,1,0:T(8,128)} copy(f32[4,128,512]{2,1,0:T(8,128)S(1)} %bitcast.8) | data formatting | bytes 2097152
